TPU v7x, 32 devices: a whole 2x2x4 slice. The times are simulated.
32 devices in a mesh: blk: 16 (over z, y, core), group: 2 (over x).
Axes of the slice: x: 2, y: 2, z: 4, core: 2. Of those that a mesh axis runs over, the one named last changes fastest.
Arguments:
- audio_embed: float32 [12288, 512], P('blk'), may hold values from -4 to 4
- text_embed: float32 [12288, 512], P(('blk', 'group')), may hold values from -4 to 4
Outputs:
- grad_audio: float32 [12288, 512], P(('blk', 'group'))
- grad_text: float32 [12288, 512], P(('blk', 'group'))
- loss_rows: float32 [12288], P(('blk', 'group'))
- loss_cols: float32 [12288], P(('blk', 'group'))
All inputs are finite; a program needn't handle non-finite values.
Results may differ from a plain program's by a relative error of at most 0.0003.
Values sent between devices are 32-bit elements; how exact they have to be, the bound alone decides.
A program may use at most 64 MiB of HBM per device.

v0:
```python
import jax
import jax.numpy as jnp
from jax import lax
from jax.sharding import PartitionSpec as P

SPAN = 3


logit_scale = 1.0 / 0.07
precise = lax.Precision.HIGHEST


def shifted(value, axis, by):
    devices = lax.axis_size(axis)
    return lax.ppermute(value, axis, [(i, (i + by) % devices) for i in range(devices)])


def merged(value, axis, join):
    pieces = jax.tree.map(lambda part: lax.all_gather(part, axis), value)
    head = jax.tree.map(lambda part: part[0], pieces)
    tail = jax.tree.map(lambda part: part[1:], pieces)
    total, _ = lax.scan(lambda total, piece: (join(total, piece), None), head, tail)
    return total


def send_ahead(payload):
    return shifted(payload, "blk", -1)


def send_back(payload):
    return shifted(payload, "blk", 1)


def pair_merge(earlier, later):
    highest = jnp.maximum(earlier[0], later[0])
    return (
        highest,
        earlier[1] * jnp.exp(earlier[0] - highest) + later[1] * jnp.exp(later[0] - highest),
    )


def shards(audio_embed, text_embed):
    row_count = audio_embed.shape[0]
    text_rows = text_embed.shape[0]
    member = lax.axis_index("group")
    text_tiles = [text_embed]
    moving = text_embed
    for _ in range(SPAN - 1):
        moving = send_ahead(moving)
        text_tiles.append(moving)
    window = jnp.stack(text_tiles)
    logits = logit_scale * jnp.einsum("rd,kcd->rkc", audio_embed, window, precision=precise)
    local_max = jnp.max(logits, axis=(1, 2))
    local_sum = jnp.sum(jnp.exp(logits - local_max[:, None, None]), axis=(1, 2))
    row_max, row_total = merged((local_max, local_sum), "group", pair_merge)
    row_lse = row_max + jnp.log(row_total)
    col_max = jnp.max(logits, axis=0)
    col_sum = jnp.sum(jnp.exp(logits - col_max[None]), axis=0)
    carried = (col_max[SPAN - 1], col_sum[SPAN - 1])
    for offset in range(SPAN - 2, -1, -1):
        arrived = send_back(carried)
        carried = pair_merge(arrived, (col_max[offset], col_sum[offset]))
    col_lse = carried[0] + jnp.log(carried[1])
    lse_tiles = [col_lse]
    moving = col_lse
    for _ in range(SPAN - 1):
        moving = send_ahead(moving)
        lse_tiles.append(moving)
    lse_window = jnp.stack(lse_tiles)
    soft_weights = 0.5 * (
        jnp.exp(logits - row_lse[:, None, None]) + jnp.exp(logits - lse_window[None])
    )
    row_ids = lax.broadcasted_iota(jnp.int32, (row_count, SPAN, text_rows), 0)
    tile_ids = lax.broadcasted_iota(jnp.int32, (row_count, SPAN, text_rows), 1)
    col_ids = lax.broadcasted_iota(jnp.int32, (row_count, SPAN, text_rows), 2)
    positive = ((tile_ids == 0) & (row_ids == member * text_rows + col_ids)).astype(jnp.float32)
    grad_logits = soft_weights - positive
    text_parts = logit_scale * jnp.einsum(
        "rkc,rd->kcd", grad_logits, audio_embed, precision=precise
    )
    grad_sum = text_parts[SPAN - 1]
    for offset in range(SPAN - 2, -1, -1):
        grad_sum = send_back(grad_sum) + text_parts[offset]
    own_logits = lax.dynamic_slice_in_dim(logits[:, 0, :], member * text_rows, text_rows, 0)
    positive_scores = jnp.diagonal(own_logits)
    own_lse = lax.dynamic_slice_in_dim(row_lse, member * text_rows, text_rows, 0)
    loss_rows = own_lse - positive_scores
    loss_cols = col_lse - positive_scores
    grad_audio = lax.psum_scatter(
        logit_scale * jnp.einsum("rkc,kcd->rd", grad_logits, window, precision=precise),
        "group",
        scatter_dimension=0,
        tiled=True,
    )
    return (grad_audio, grad_sum, loss_rows, loss_cols)


def solution(mesh):
    placed = (P("blk", None), P(("blk", "group"), None))
    return jax.shard_map(
        shards,
        mesh=mesh,
        in_specs=placed,
        out_specs=(
            P(("blk", "group"), None),
            P(("blk", "group"), None),
            P(("blk", "group")),
            P(("blk", "group")),
        ),
        check_vma=False,
    )
```

profile of v0, /device:TPU:0, one launch (start us, length us, event | category | flops | bytes accessed | tf_op | source)
XLA Modules:
  0.0 128.4 jit_solution(6770058286983946812)
XLA Ops:
  7.2 5.5 %collective-permute-start = (f32[384,512]{1,0:T(8,128)}, f32[384,512]{1,0:T(8,128)S(1)}, u32[]{:S(2)}, u32[]{:S(2)}) collective-permute-start(f32[384,512]{1,0:T(8,128)} %param.3), channel_id=1, source_target_pairs={{0,30},{2,0},{4,2},{6,4},{8,6},{10,8},{12,10},{14,12},{16,14},{18,... | collective-permute-start | bytes 2359304 | tf_op jit(solution)/shard_map/ppermute | solution.py:15
  12.7 9.8 %collective-permute-done = f32[384,512]{1,0:T(8,128)S(1)} collective-permute-done((f32[384,512]{1,0:T(8,128)}, f32[384,512]{1,0:T(8,128)S(1)}, u32[]{:S(2)}, u32[]{:S(2)}) %collective-permute-start) | collective-permute-done | bytes 786464 | tf_op jit(solution)/shard_map/ppermute | solution.py:15
  22.5 4.5 %collective-permute-start.1 = (f32[384,512]{1,0:T(8,128)S(1)}, f32[384,512]{1,0:T(8,128)S(1)}, u32[]{:S(2)}, u32[]{:S(2)}) collective-permute-start(f32[384,512]{1,0:T(8,128)S(1)} %collective-permute-done), channel_id=1, source_target_pairs={{0,30},{2,0},{4,2},{6,4},{8,6},{10,8},{12,10},{14,12},{16,14},{18,... | collective-permute-start | bytes 2359304 | tf_op jit(solution)/shard_map/ppermute | solution.py:15
  27.1 9.5 %collective-permute-done.1 = f32[384,512]{1,0:T(8,128)S(1)} collective-permute-done((f32[384,512]{1,0:T(8,128)S(1)}, f32[384,512]{1,0:T(8,128)S(1)}, u32[]{:S(2)}, u32[]{:S(2)}) %collective-permute-start.1) | collective-permute-done | bytes 786464 | tf_op jit(solution)/shard_map/ppermute | solution.py:15
  36.6 7.6 %fusion.2 = f32[3,384,768]{2,1,0:T(8,128)S(1)} fusion(f32[1,384,512]{2,1,0:T(8,128)S(1)} %bitcast.40, f32[1,384,512]{2,1,0:T(8,128)S(1)} %bitcast.38, f32[1,384,512]{2,1,0:T(8,128)} %bitcast.36, f32[768,512]{1,0:T(8,128)S(1)} %copy-done), kind=kOutput, calls=%fused_computation.11 | convolution fusion | flops 5436997632 | bytes 7471104 | tf_op jit(solution)/shard_map/rd,kcd->rkc/dot_general | solution.py:52
  44.2 0.5 multiply_reduce_fusion
  44.7 1.1 exponential_reduce_fusion.1
  45.8 0.2 copy-done.1
  46.0 0.8 exponential_reduce_fusion
  47.0 4.5 %all-gather.3 = f32[2,1,768]{2,1,0:T(1,128)S(1)} all-gather(f32[1,1,768]{2,1,0:T(1,128)S(1)} %reshape.62), channel_id=3, replica_groups=mesh['blk'=16,'group'=2] {'group'}, dimensions={0}, use_global_device_ids=true | all-gather | bytes 9216 | tf_op jit(solution)/shard_map/all_gather | solution.py:19
  51.5 4.3 %all-gather.2 = f32[2,1,768]{2,1,0:T(1,128)S(1)} all-gather(f32[1,1,768]{2,1,0:T(1,128)S(1)} %reshape.60), channel_id=2, replica_groups=mesh['blk'=16,'group'=2] {'group'}, dimensions={0}, use_global_device_ids=true | all-gather | bytes 9216 | tf_op jit(solution)/shard_map/all_gather | solution.py:19
  56.2 3.5 %gather_fusion = f32[384]{0:T(512)S(1)} fusion(f32[384,384]{0,1:T(8,128)S(1)} %dynamic-slice_bitcast_fusion, s32[384]{0:T(512)S(1)} %or_reduce_fusion), kind=kCustom, calls=%fused_computation | custom fusion | bytes 6144 | tf_op jit(solution)/shard_map/jit(diagonal)/cond/branch_0_fun/gather | solution.py:85
  59.7 2.1 %collective-permute-done.5 = f32[384]{0:T(512)S(1)} collective-permute-done((f32[384]{0:T(512)S(1)}, f32[384]{0:T(512)S(1)}, u32[]{:S(2)}, u32[]{:S(2)}) %collective-permute-start.5) | collective-permute-done | bytes 1568 | tf_op jit(solution)/shard_map/ppermute | solution.py:15
  61.9 0.7 fusion.14
  62.5 2.3 %collective-permute-start.6 = (f32[384]{0:T(512)S(1)}, f32[384]{0:T(512)S(1)}, u32[]{:S(2)}, u32[]{:S(2)}) collective-permute-start(f32[384]{0:T(512)S(1)} %get-tuple-element.32), channel_id=1, source_target_pairs={{0,30},{2,0},{4,2},{6,4},{8,6},{10,8},{12,10},{14,12},{16,14},{18,... | collective-permute-start | bytes 4616 | tf_op jit(solution)/shard_map/ppermute | solution.py:15
  64.8 1.3 %collective-permute-done.6 = f32[384]{0:T(512)S(1)} collective-permute-done((f32[384]{0:T(512)S(1)}, f32[384]{0:T(512)S(1)}, u32[]{:S(2)}, u32[]{:S(2)}) %collective-permute-start.6) | collective-permute-done | bytes 1568 | tf_op jit(solution)/shard_map/ppermute | solution.py:15
  66.1 4.4 %collective-permute-start.7 = (f32[384]{0:T(512)S(1)}, f32[384]{0:T(512)S(1)}, u32[]{:S(2)}, u32[]{:S(2)}) collective-permute-start(f32[384]{0:T(512)S(1)} %collective-permute-done.6), channel_id=1, source_target_pairs={{0,30},{2,0},{4,2},{6,4},{8,6},{10,8},{12,10},{14,12},{16,14},{18,... | collective-permute-start | bytes 4616 | tf_op jit(solution)/shard_map/ppermute | solution.py:15
  70.5 1.3 %collective-permute-done.7 = f32[384]{0:T(512)S(1)} collective-permute-done((f32[384]{0:T(512)S(1)}, f32[384]{0:T(512)S(1)}, u32[]{:S(2)}, u32[]{:S(2)}) %collective-permute-start.7) | collective-permute-done | bytes 1568 | tf_op jit(solution)/shard_map/ppermute | solution.py:15
  71.8 11.0 %bitcast_multiply_fusion = f32[768,512]{1,0:T(8,128)} fusion(f32[1,384,512]{2,1,0:T(8,128)} %bitcast.41, f32[1,384,512]{2,1,0:T(8,128)} %bitcast.39, f32[1,384,512]{2,1,0:T(8,128)S(1)} %bitcast.37, s32[384]{0:T(512)S(1)} %iota_add_fusion, f32[3,384]{1,0:T(4,128)S(1)} %pad_maximum_fusion.5, f32[768]{0:T(1024)S(1)} %log_add_fusion, ...), kind=kOutput, calls=%fused_computation.12 | convolution fusion | flops 5445353472 | bytes 7480323 | tf_op jit(solution)/shard_map/rkc,kcd->rd/dot_general | solution.py:90
  82.9 9.1 %convolution_multiply_fusion = f32[3,384,512]{2,1,0:T(8,128)S(1)} fusion(f32[768,512]{1,0:T(8,128)S(1)} %copy-done, s32[384]{0:T(512)S(1)} %iota_add_fusion, f32[3,384]{1,0:T(4,128)S(1)} %pad_maximum_fusion.5, f32[768]{0:T(1024)S(1)} %log_add_fusion, pred[3]{0:T(512)(128)(4,1)S(1)} %iota_compare_fusion.1, f32[3,384,768]{2,1,0:T(8,128)} %copy-done.1), kind=kOutput, calls=%fused_computation.9 | convolution fusion | flops 5444370432 | bytes 7480323 | tf_op jit(solution)/shard_map/rkc,rd->kcd/dot_general | solution.py:78
  92.1 14.1 %collective-permute-done.8 = f32[384,512]{1,0:T(8,128)S(1)} collective-permute-done((f32[384,512]{1,0:T(8,128)S(1)}, f32[384,512]{1,0:T(8,128)S(1)}, u32[]{:S(2)}, u32[]{:S(2)}) %collective-permute-start.8) | collective-permute-done | bytes 786464 | tf_op jit(solution)/shard_map/ppermute | solution.py:15
  106.2 0.1 fusion.6
  106.5 14.1 %collective-permute-done.9 = f32[384,512]{1,0:T(8,128)S(1)} collective-permute-done((f32[384,512]{1,0:T(8,128)S(1)}, f32[384,512]{1,0:T(8,128)S(1)}, u32[]{:S(2)}, u32[]{:S(2)}) %collective-permute-start.9) | collective-permute-done | bytes 786464 | tf_op jit(solution)/shard_map/ppermute | solution.py:15
  120.6 1.0 fusion.5
  (39 shorter events, 0.9 us)
Async XLA Ops:
  7.2 29.4 %copy-start = (f32[768,512]{1,0:T(8,128)S(1)}, f32[768,512]{1,0:T(8,128)}, u32[]{:S(2)}) copy-start(f32[768,512]{1,0:T(8,128)} %param.2) | copy-start | bytes 4718596
  7.2 114.4 %reduce-scatter.2.cloned.1.call-start = ((), (), s32[]{:S(2)}) async-start(), calls=%async_computation.1 | async-start | bytes 2359296 | tf_op jit(solution)/shard_map/reduce_scatter | solution.py:89
  7.2 15.3 %collective-permute-start = (f32[384,512]{1,0:T(8,128)}, f32[384,512]{1,0:T(8,128)S(1)}, u32[]{:S(2)}, u32[]{:S(2)}) collective-permute-start(f32[384,512]{1,0:T(8,128)} %param.3), channel_id=1, source_target_pairs={{0,30},{2,0},{4,2},{6,4},{8,6},{10,8},{12,10},{14,12},{16,14},{18,... | collective-permute-start | bytes 2359304 | tf_op jit(solution)/shard_map/ppermute | solution.py:15
  22.5 21.6 %copy-start.3 = (f32[384,512]{1,0:T(8,128)}, f32[384,512]{1,0:T(8,128)S(1)}, u32[]{:S(2)}) copy-start(f32[384,512]{1,0:T(8,128)S(1)} %collective-permute-done) | copy-start | bytes 2359300
  22.5 14.0 %collective-permute-start.1 = (f32[384,512]{1,0:T(8,128)S(1)}, f32[384,512]{1,0:T(8,128)S(1)}, u32[]{:S(2)}, u32[]{:S(2)}) collective-permute-start(f32[384,512]{1,0:T(8,128)S(1)} %collective-permute-done), channel_id=1, source_target_pairs={{0,30},{2,0},{4,2},{6,4},{8,6},{10,8},{12,10},{14,12},{16,14},{18,... | collective-permute-start | bytes 2359304 | tf_op jit(solution)/shard_map/ppermute | solution.py:15
  36.6 7.7 %copy-start.4 = (f32[384,512]{1,0:T(8,128)}, f32[384,512]{1,0:T(8,128)S(1)}, u32[]{:S(2)}) copy-start(f32[384,512]{1,0:T(8,128)S(1)} %collective-permute-done.1) | copy-start | bytes 2359300
  44.2 1.8 %copy-start.1 = (f32[3,384,768]{2,1,0:T(8,128)}, f32[3,384,768]{2,1,0:T(8,128)S(1)}, u32[]{:S(2)}) copy-start(f32[3,384,768]{2,1,0:T(8,128)S(1)} %fusion.2) | copy-start | bytes 10616836
  46.8 25.0 %copy-start.2 = (f32[384,512]{1,0:T(8,128)S(1)}, f32[384,512]{1,0:T(8,128)}, u32[]{:S(2)}) copy-start(f32[384,512]{1,0:T(8,128)} %param.3) | copy-start | bytes 2359300
  46.9 9.1 %collective-permute-start.4 = (f32[384]{0:T(512)S(1)}, f32[384]{0:T(512)S(1)}, u32[]{:S(2)}, u32[]{:S(2)}) collective-permute-start(f32[384]{0:T(512)S(1)} %get-tuple-element.25), channel_id=1, source_target_pairs={{0,2},{2,4},{4,6},{6,8},{8,10},{10,12},{12,14},{14,16},{16,18},{18... | collective-permute-start | bytes 4616 | tf_op jit(solution)/shard_map/ppermute | solution.py:15
  46.9 9.1 %collective-permute-start.2 = (f32[384]{0:T(512)S(1)}, f32[384]{0:T(512)S(1)}, u32[]{:S(2)}, u32[]{:S(2)}) collective-permute-start(f32[384]{0:T(512)S(1)} %get-tuple-element.30), channel_id=1, source_target_pairs={{0,2},{2,4},{4,6},{6,8},{8,10},{10,12},{12,14},{14,16},{16,18},{18... | collective-permute-start | bytes 4616 | tf_op jit(solution)/shard_map/ppermute | solution.py:15
  56.0 5.8 %collective-permute-start.5 = (f32[384]{0:T(512)S(1)}, f32[384]{0:T(512)S(1)}, u32[]{:S(2)}, u32[]{:S(2)}) collective-permute-start(f32[384]{0:T(512)S(1)} %get-tuple-element.33), channel_id=1, source_target_pairs={{0,2},{2,4},{4,6},{6,8},{8,10},{10,12},{12,14},{14,16},{16,18},{18... | collective-permute-start | bytes 4616 | tf_op jit(solution)/shard_map/ppermute | solution.py:15
  56.1 5.8 %collective-permute-start.3 = (f32[384]{0:T(512)S(1)}, f32[384]{0:T(512)S(1)}, u32[]{:S(2)}, u32[]{:S(2)}) collective-permute-start(f32[384]{0:T(512)S(1)} %get-tuple-element.34), channel_id=1, source_target_pairs={{0,2},{2,4},{4,6},{6,8},{8,10},{10,12},{12,14},{14,16},{16,18},{18... | collective-permute-start | bytes 4616 | tf_op jit(solution)/shard_map/ppermute | solution.py:15
  62.5 3.6 %collective-permute-start.6 = (f32[384]{0:T(512)S(1)}, f32[384]{0:T(512)S(1)}, u32[]{:S(2)}, u32[]{:S(2)}) collective-permute-start(f32[384]{0:T(512)S(1)} %get-tuple-element.32), channel_id=1, source_target_pairs={{0,30},{2,0},{4,2},{6,4},{8,6},{10,8},{12,10},{14,12},{16,14},{18,... | collective-permute-start | bytes 4616 | tf_op jit(solution)/shard_map/ppermute | solution.py:15
  66.1 5.7 %collective-permute-start.7 = (f32[384]{0:T(512)S(1)}, f32[384]{0:T(512)S(1)}, u32[]{:S(2)}, u32[]{:S(2)}) collective-permute-start(f32[384]{0:T(512)S(1)} %collective-permute-done.6), channel_id=1, source_target_pairs={{0,30},{2,0},{4,2},{6,4},{8,6},{10,8},{12,10},{14,12},{16,14},{18,... | collective-permute-start | bytes 4616 | tf_op jit(solution)/shard_map/ppermute | solution.py:15
  92.1 14.2 %collective-permute-start.8 = (f32[384,512]{1,0:T(8,128)S(1)}, f32[384,512]{1,0:T(8,128)S(1)}, u32[]{:S(2)}, u32[]{:S(2)}) collective-permute-start(f32[384,512]{1,0:T(8,128)S(1)} %slice_bitcast_fusion.2), channel_id=1, source_target_pairs={{0,2},{2,4},{4,6},{6,8},{8,10},{10,12},{12,14},{14,16},{16,18},{18... | collective-permute-start | bytes 2359304 | tf_op jit(solution)/shard_map/ppermute | solution.py:15
  106.4 14.2 %collective-permute-start.9 = (f32[384,512]{1,0:T(8,128)S(1)}, f32[384,512]{1,0:T(8,128)S(1)}, u32[]{:S(2)}, u32[]{:S(2)}) collective-permute-start(f32[384,512]{1,0:T(8,128)S(1)} %fusion.6), channel_id=1, source_target_pairs={{0,2},{2,4},{4,6},{6,8},{8,10},{10,12},{12,14},{14,16},{16,18},{18... | collective-permute-start | bytes 2359304 | tf_op jit(solution)/shard_map/ppermute | solution.py:15
Sparse Core Ops, SparseCore 0:
  83.0 27.1 reduce-scatter.1
where the time goes:
time: 129 us; the launch traced here: 128 us
  waiting for transfers between devices  52.3 us (41%)
  matrix products  27.8 us (22%)
  starting transfers between devices  17 us (13%)
  between operations  14.2 us (11%)
  blocking collectives  8.81 us (7%)
  other arithmetic  4.31 us (3%)
  local copies, waits for them, and re-layouts  3.94 us (3%)
    ppermute x10, waiting for transfers between devices, shifted(): lax.ppermute(value, axis, [(i, (i + by) % devices) for i in range(devices)])  52.3 us
    ppermute x10, starting transfers between devices, shifted(): lax.ppermute(value, axis, [(i, (i + by) % devices) for i in range(devices)])  17 us
    dot_general x1, matrix products, shards(): jnp.einsum('rkc,kcd->rd', grad_logits, window, precision=precise)  11 us
    dot_general x1, matrix products, shards(): jnp.einsum('rkc,rd->kcd', grad_logits, audio_embed, precision=precise)  9.12 us
    all_gather x2, blocking collectives, merged(): pieces = jax.tree.map(lambda part: lax.all_gather(part, axis), value)  8.81 us
    dot_general x1, matrix products, shards(): jnp.einsum('rd,kcd->rkc', audio_embed, window, precision=precise)  7.63 us
    gather x1, local copies, waits for them, and re-layouts, shards(): positive_scores = jnp.diagonal(own_logits)  3.47 us
  transfers between devices with their start and end apart: 11, of which 8 were waited for; matrix products, arithmetic and copies ran while one was open for 11% of the time, Pallas kernels for 0%

commit v1 on v0

v1 whole, which is shorter than its diff:
```python
import functools
import math

import jax
import jax.numpy as jnp
from jax import lax
from jax.experimental import pallas as pl
from jax.experimental.pallas import tpu as pltpu
from jax.sharding import PartitionSpec as P

SPAN = 3
LANES = 128
MESH = pl.DeviceIdType.MESH

logit_scale = 1.0 / 0.07
log2e = math.log2(math.e)
ln2 = math.log(2.0)
bf16 = jnp.bfloat16
f32 = jnp.float32


def split(value):
    high = value.astype(bf16)
    return high, (value - high.astype(f32)).astype(bf16)


def dot(a, b):
    return jnp.dot(a, b, preferred_element_type=f32)


def dot3(a_high, a_low, b_high, b_low):
    return dot(a_high, b_high) + dot(a_high, b_low) + dot(a_low, b_high)


def merge(first, second):
    highest = jnp.maximum(first[0], second[0])
    return (
        highest,
        first[1] * jnp.exp2(first[0] - highest) + second[1] * jnp.exp2(second[0] - highest),
    )


def kernel(
    n_blk, n_group, parts,
    audio, text,
    grad_audio, grad_text, loss_rows, loss_cols,
    window, audio_high, audio_low, turned_high, turned_low,
    text_turned_high, text_turned_low, logits, g_high, g_low,
    audio_part, audio_inbox,
    text_part, inbox, relay,
    tall, wide, col_box, row_box, row_stat,
    fwd_send, fwd_recv, stat_send, stat_recv, row_send, row_recv,
    back_send, back_recv, ga_send, ga_recv,
):
    rows, depth = audio.shape
    cols = text.shape[0]
    chunk = cols // parts
    padded = wide.shape[2]
    b = lax.axis_index("blk")
    member = lax.axis_index("group")
    odd = lax.rem(b, 2) == 1
    even = lax.rem(b, 2) == 0

    def at(step, group=None):
        return {
            "blk": lax.rem(b + step + n_blk, n_blk),
            "group": member if group is None else group,
        }

    def peer(step):
        return lax.rem(member + step, n_group)

    barrier = pltpu.get_barrier_semaphore()
    for step in (-2, -1, 1, 2):
        pl.semaphore_signal(barrier, inc=1, device_id=at(step), device_id_type=MESH)
    for step in range(1, n_group):
        pl.semaphore_signal(barrier, inc=1, device_id=at(0, peer(step)), device_id_type=MESH)
    pl.semaphore_wait(barrier, 4 + n_group - 1)

    def piece(c):
        return pl.ds(c * chunk, chunk)

    def remote(src, dst, send, recv, device):
        return pltpu.make_async_remote_copy(
            src_ref=src, dst_ref=dst, send_sem=send, recv_sem=recv,
            device_id=device, device_id_type=MESH,
        )

    def near(c):
        return remote(text.at[piece(c)], window.at[0, piece(c)], fwd_send.at[0, c], fwd_recv.at[0, c], at(-1))

    def far(c):
        return remote(text.at[piece(c)], window.at[1, piece(c)], fwd_send.at[1, c], fwd_recv.at[1, c], at(-2))

    def pass_on(c):
        return remote(
            window.at[0, piece(c)], window.at[1, piece(c)], fwd_send.at[2, c], fwd_recv.at[1, c], at(-1)
        )

    for c in range(parts):
        near(c).start()
    for c in range(parts):
        @pl.when(odd)
        def _():
            far(c).start()

    scaled = audio[...] * (logit_scale * log2e)
    high, low = split(scaled)
    audio_high[...] = high
    audio_low[...] = low
    turned = scaled.T
    high, low = split(turned)
    turned_high[...] = high
    turned_low[...] = low
    tall[...] = jnp.zeros_like(tall)
    row_stat[...] = jnp.zeros_like(row_stat)

    ids_text = lax.broadcasted_iota(jnp.int32, (chunk, rows), 0)
    ids_audio = lax.broadcasted_iota(jnp.int32, (chunk, rows), 1)

    def positive(c):
        return ids_audio == ids_text + (member * cols + c * chunk)

    lane = lax.broadcasted_iota(jnp.int32, (chunk, LANES), 1)

    def stat_copy(mine, theirs):
        return remote(
            wide.at[mine], col_box.at[theirs, mine],
            stat_send.at[theirs, mine], stat_recv.at[theirs, mine], at(mine - theirs),
        )

    for k in range(SPAN):
        for c in range(parts):
            if k == 0:
                block = text[piece(c)]
            else:
                if k == 1:
                    near(c).wait_recv()

                    @pl.when(odd)
                    def _():
                        pass_on(c).start()
                else:
                    far(c).wait_recv()
                block = window[k - 1, piece(c)]
            high, low = split(block)
            start = k * cols + c * chunk
            tile = dot3(high, low, turned_high[...], turned_low[...])
            logits[pl.ds(start, chunk)] = tile
            top = jnp.max(tile, axis=1, keepdims=True)
            total = jnp.sum(jnp.exp2(tile - top), axis=1, keepdims=True)
            tall[piece(c)] = jnp.where(lane == 0, top, total)
            top = jnp.max(tile, axis=0, keepdims=True)
            if start:
                top = jnp.maximum(top, row_stat[0:1])
            total = jnp.sum(jnp.exp2(tile - top), axis=0, keepdims=True)
            if start:
                total = total + row_stat[1:2] * jnp.exp2(row_stat[0:1] - top)
            row_stat[0:1] = top
            row_stat[1:2] = total
        wide[k] = tall[...].T[0:8]
        for theirs in range(SPAN):
            if theirs != k:
                stat_copy(k, theirs).start()
        if k == SPAN - 1:
            for step in range(1, n_group):
                remote(
                    row_stat, row_box.at[step], row_send.at[step], row_recv.at[step], at(0, peer(step))
                ).start()
        block = text[...] if k == 0 else window[k - 1]
        high, low = split(block.T)
        text_turned_high[k] = high
        text_turned_low[k] = low

    pair = (row_stat[0:1], row_stat[1:2])
    for step in range(1, n_group):
        remote(
            row_stat, row_box.at[step], row_send.at[step], row_recv.at[step], at(0, peer(step))
        ).wait_recv()
        pair = merge(pair, (row_box[step, 0:1], row_box[step, 1:2]))
    row_lse = pair[0] + jnp.log2(pair[1])

    def back(k, c):
        part = text_part.at[k, piece(c)]
        if k == 2:
            return (
                remote(part, inbox.at[1, piece(c)], back_send.at[1, c], back_recv.at[1, c], at(2)),
                remote(part, relay.at[piece(c)], back_send.at[1, c], back_recv.at[2, c], at(1)),
            )
        return remote(part, inbox.at[0, piece(c)], back_send.at[0, c], back_recv.at[0, c], at(1))

    def weights(k):
        pair = (wide[k, 0:1], wide[k, 1:2])
        for other in range(SPAN):
            if other != k:
                stat_copy(other, k).wait_recv()
                pair = merge(pair, (col_box[k, other, 0:1], col_box[k, other, 1:2]))
        col_lse = jnp.broadcast_to(pair[0] + jnp.log2(pair[1]), (LANES, padded)).T
        for c in range(parts):
            start = k * cols + c * chunk
            tile = logits[pl.ds(start, chunk)]
            own_lse = col_lse[c * chunk:(c + 1) * chunk, 0:1]
            weight = 0.5 * (jnp.exp2(tile - row_lse) + jnp.exp2(tile - own_lse))
            if k == 0:
                here = positive(c)
                weight = jnp.where(here, weight - 1.0, weight)
                score = jnp.sum(jnp.where(here, tile, 0.0), axis=1, keepdims=True)
                own_row = jnp.sum(jnp.where(here, row_lse, 0.0), axis=1, keepdims=True)
                tall[piece(c)] = ln2 * jnp.where(lane == 0, own_row - score, own_lse - score)
            high, low = split(weight)
            g_high[pl.ds(start, chunk)] = high
            g_low[pl.ds(start, chunk)] = low

    def text_terms(k, c):
        here = pl.ds(k * cols + c * chunk, chunk)
        return ln2 * dot3(g_high[here], g_low[here], audio_high[...], audio_low[...])

    weights(2)
    for c in range(parts):
        text_part[2, piece(c)] = text_terms(2, c)

        @pl.when(odd)
        def _():
            back(2, c)[0].start()

        @pl.when(even)
        def _():
            back(2, c)[1].start()

    weights(1)
    for c in range(parts):
        text_part[1, piece(c)] = text_terms(1, c)

        @pl.when(odd)
        def _():
            back(2, c)[1].wait_recv()
            text_part[1, piece(c)] += relay[piece(c)]

        back(1, c).start()

    weights(0)
    losses = tall[...].T
    loss_rows[...] = losses[0:1, 0:cols]
    loss_cols[...] = losses[1:2, 0:cols]

    span = 256 if rows % 256 == 0 else rows
    for start in range(0, rows, span):
        total = None
        for k in range(SPAN):
            here = (pl.ds(k * cols, cols), pl.ds(start, span))
            term = dot3(text_turned_high[k], text_turned_low[k], g_high[here], g_low[here])
            total = term if total is None else total + term
        audio_part[pl.ds(start, span)] = logit_scale * total.T

    def share(group):
        return pl.ds(pl.multiple_of(group * cols, 8), cols)

    def spread(step):
        return remote(
            audio_part.at[share(peer(step))], audio_inbox.at[step],
            ga_send.at[step], ga_recv.at[step], at(0, peer(step)),
        )

    for step in range(1, n_group):
        spread(step).start()

    for c in range(parts):
        text_part[0, piece(c)] = text_terms(0, c)

    total = audio_part[share(member)]
    for step in range(1, n_group):
        spread(step).wait_recv()
        total = total + audio_inbox[step]
    grad_audio[...] = total

    for c in range(parts):
        back(1, c).wait_recv()
        grad_text[piece(c)] = text_part[0, piece(c)] + inbox[0, piece(c)]

        @pl.when(odd)
        def _():
            back(2, c)[0].wait_recv()
            grad_text[piece(c)] += inbox[1, piece(c)]

    for c in range(parts):
        near(c).wait_send()
        back(2, c)[0].wait_send()
        back(1, c).wait_send()

        @pl.when(odd)
        def _():
            far(c).wait_send()
            pass_on(c).wait_send()

    for mine in range(SPAN):
        for theirs in range(SPAN):
            if mine != theirs:
                stat_copy(mine, theirs).wait_send()
    for step in range(1, n_group):
        remote(
            row_stat, row_box.at[step], row_send.at[step], row_recv.at[step], at(0, peer(step))
        ).wait_send()
        spread(step).wait_send()


def shards(n_blk, n_group, audio_embed, text_embed):
    rows, depth = audio_embed.shape
    cols = text_embed.shape[0]
    parts = 2
    padded = -(-cols // LANES) * LANES
    vmem = pl.BlockSpec(memory_space=pltpu.VMEM)
    dma = pltpu.SemaphoreType.DMA
    grad_audio, grad_text, loss_rows, loss_cols = pl.pallas_call(
        functools.partial(kernel, n_blk, n_group, parts),
        out_shape=(
            jax.ShapeDtypeStruct((cols, depth), f32),
            jax.ShapeDtypeStruct((cols, depth), f32),
            jax.ShapeDtypeStruct((1, cols), f32),
            jax.ShapeDtypeStruct((1, cols), f32),
        ),
        in_specs=[vmem, vmem],
        out_specs=(vmem, vmem, vmem, vmem),
        scratch_shapes=[
            pltpu.VMEM((SPAN - 1, cols, depth), f32),
            pltpu.VMEM((rows, depth), bf16),
            pltpu.VMEM((rows, depth), bf16),
            pltpu.VMEM((depth, rows), bf16),
            pltpu.VMEM((depth, rows), bf16),
            pltpu.VMEM((SPAN, depth, cols), bf16),
            pltpu.VMEM((SPAN, depth, cols), bf16),
            pltpu.VMEM((SPAN * cols, rows), f32),
            pltpu.VMEM((SPAN * cols, rows), bf16),
            pltpu.VMEM((SPAN * cols, rows), bf16),
            pltpu.VMEM((rows, depth), f32),
            pltpu.VMEM((n_group, cols, depth), f32),
            pltpu.VMEM((SPAN, cols, depth), f32),
            pltpu.VMEM((2, cols, depth), f32),
            pltpu.VMEM((cols, depth), f32),
            pltpu.VMEM((padded, LANES), f32),
            pltpu.VMEM((SPAN, 8, padded), f32),
            pltpu.VMEM((SPAN, SPAN, 8, padded), f32),
            pltpu.VMEM((n_group, 8, rows), f32),
            pltpu.VMEM((8, rows), f32),
            dma((3, parts)), dma((2, parts)),
            dma((SPAN, SPAN)), dma((SPAN, SPAN)),
            dma((n_group,)), dma((n_group,)),
            dma((2, parts)), dma((3, parts)),
            dma((n_group,)), dma((n_group,)),
        ],
        compiler_params=pltpu.CompilerParams(
            collective_id=0, has_side_effects=True, vmem_limit_bytes=56 * 1024 * 1024
        ),
        name="contrast",
    )(audio_embed, text_embed)
    return grad_audio, grad_text, loss_rows.reshape(cols), loss_cols.reshape(cols)


def solution(mesh):
    return jax.shard_map(
        functools.partial(shards, mesh.shape["blk"], mesh.shape["group"]),
        mesh=mesh,
        in_specs=(P("blk", None), P(("blk", "group"), None)),
        out_specs=(
            P(("blk", "group"), None),
            P(("blk", "group"), None),
            P(("blk", "group")),
            P(("blk", "group")),
        ),
        check_vma=False,
    )
```

time: 129 us -> 68 us (0.53)
  Pallas kernels: 0 us -> 61.6 us
  waiting for transfers between devices: 52.3 us -> 0 us
  matrix products: 27.8 us -> 0 us
  starting transfers between devices: 17 us -> 0 us
  between operations: 14.2 us -> 0.65 us
  blocking collectives: 8.81 us -> 0 us
  other arithmetic: 4.31 us -> 2.6 us
    pallas_call x0 -> x1, Pallas kernels: none -> 61.6 us  [shards(): pl.pallas_call(functools.partial(kernel, n_blk, n_group, parts), out_shap...]
    ppermute x10 -> x0, waiting for transfers between devices: 52.3 us -> none  [shifted(): lax.ppermute(value, axis, [(i, (i + by) % devices) for i in range(devices)])]
    dot_general x3 -> x0, matrix products: 27.8 us -> none  [the longest x1 11 us: shards(): jnp.einsum('rkc,kcd->rd', grad_logits, window, precision=precise)]
    ppermute x10 -> x0, starting transfers between devices: 17 us -> none  [shifted(): lax.ppermute(value, axis, [(i, (i + by) % devices) for i in range(devices)])]
    all_gather x2 -> x0, blocking collectives: 8.81 us -> none  [merged(): pieces = jax.tree.map(lambda part: lax.all_gather(part, axis), value)]
    gather x1 -> x0, local copies, waits for them, and re-layouts: 3.47 us -> none  [shards(): positive_scores = jnp.diagonal(own_logits)]
    unnamed x12 -> x4, local copies, waits for them, and re-layouts: 0.18 us -> 2.95 us
    pallas_call x0 -> x2, other arithmetic: none -> 2.6 us  [shards(): pl.pallas_call(functools.partial(kernel, n_blk, n_group, parts), out_shap...]
  transfers between devices with their start and end apart: 11 -> 0, of which waited for: 8 -> 0; matrix products, arithmetic and copies ran while one was open for 11% -> 0% of each run, Pallas kernels for 0% -> 0%
where the time goes in v1:
time: 68 us; the launch traced here: 67.7 us
  Pallas kernels  61.6 us (91%)
  local copies, waits for them, and re-layouts  2.95 us (4%)
  other arithmetic  2.6 us (4%)
    pallas_call x1, Pallas kernels, shards(): pl.pallas_call(functools.partial(kernel, n_blk, n_group, parts), out_shap...  61.6 us
    unnamed x4, local copies, waits for them, and re-layouts  2.95 us
    pallas_call x2, other arithmetic, shards(): pl.pallas_call(functools.partial(kernel, n_blk, n_group, parts), out_shap...  2.6 us

profile of v1, /device:TPU:0, one launch (start us, length us, event | category | flops | bytes accessed | tf_op | source)
XLA Modules:
  0.0 67.7 jit_solution(10685100662903699547)
XLA Ops:
  0.6 61.6 %contrast.1 = (f32[384,512]{1,0:T(8,128)}, f32[384,512]{1,0:T(8,128)}, f32[1,384]{1,0:T(1,128)}, f32[1,384]{1,0:T(1,128)}) custom-call(f32[768,512]{1,0:T(8,128)} %audio.1, f32[384,512]{1,0:T(8,128)} %text.1), custom_call_target="tpu_custom_call" | custom-call | tf_op jit(solution)/shard_map/contrast/pallas_call | solution.py:313
  62.2 0.0 copy-start
  62.2 1.3 %reduce = f32[384]{0:T(512)} reduce(f32[1,384]{1,0:T(1,128)} %get-tuple-element.10, f32[]{:T(128)} %constant), dimensions={0}, to_apply=%get-tuple-element.10.reduce_sub_computation | reduce | bytes 3076 | tf_op jit(solution)/shard_map/contrast/pallas_call | solution.py:313
  63.5 1.3 %reduce.1 = f32[384]{0:T(512)} reduce(f32[1,384]{1,0:T(1,128)} %get-tuple-element.11, f32[]{:T(128)} %constant), dimensions={0}, to_apply=%get-tuple-element.11.reduce_sub_computation | reduce | bytes 3076 | tf_op jit(solution)/shard_map/contrast/pallas_call | solution.py:313
  64.8 2.1 %copy.8 = f32[384,512]{1,0:T(8,128)} copy(f32[384,512]{1,0:T(8,128)} %get-tuple-element.16) | data formatting | bytes 1572864
  66.9 0.0 copy-done
  66.9 0.9 %copy.9 = f32[384,512]{1,0:T(8,128)} copy(f32[384,512]{1,0:T(8,128)S(1)} %copy-done) | data formatting | bytes 1572864
Async XLA Ops:
  62.2 4.7 %copy-start = (f32[384,512]{1,0:T(8,128)S(1)}, f32[384,512]{1,0:T(8,128)}, u32[]{:S(2)}) copy-start(f32[384,512]{1,0:T(8,128)} %get-tuple-element.17) | copy-start | bytes 2359300

commit v2 on v1

--- a/solution.py
+++ b/solution.py
@@ -41,7 +41,7 @@
 
 
 def kernel(
-    n_blk, n_group, parts,
+    n_blk, n_group, parts, steps,
     audio, text,
     grad_audio, grad_text, loss_rows, loss_cols,
     window, audio_high, audio_low, turned_high, turned_low,
@@ -55,6 +55,7 @@
     rows, depth = audio.shape
     cols = text.shape[0]
     chunk = cols // parts
+    strip = cols // steps
     padded = wide.shape[2]
     b = lax.axis_index("blk")
     member = lax.axis_index("group")
@@ -99,11 +100,6 @@
 
     for c in range(parts):
         near(c).start()
-    for c in range(parts):
-        @pl.when(odd)
-        def _():
-            far(c).start()
-
     scaled = audio[...] * (logit_scale * log2e)
     high, low = split(scaled)
     audio_high[...] = high
@@ -115,11 +111,10 @@
     tall[...] = jnp.zeros_like(tall)
     row_stat[...] = jnp.zeros_like(row_stat)
 
-    ids_text = lax.broadcasted_iota(jnp.int32, (chunk, rows), 0)
-    ids_audio = lax.broadcasted_iota(jnp.int32, (chunk, rows), 1)
-
     def positive(c):
-        return ids_audio == ids_text + (member * cols + c * chunk)
+        ids_text = lax.broadcasted_iota(jnp.int32, (strip, rows), 0)
+        ids_audio = lax.broadcasted_iota(jnp.int32, (strip, rows), 1)
+        return ids_audio == ids_text + (member * cols + c * strip)
 
     lane = lax.broadcasted_iota(jnp.int32, (chunk, LANES), 1)
 
@@ -130,6 +125,11 @@
         )
 
     for k in range(SPAN):
+        if k == 1:
+            @pl.when(odd)
+            def _():
+                far(0).start()
+
         for c in range(parts):
             if k == 0:
                 block = text[piece(c)]
@@ -140,6 +140,8 @@
                     @pl.when(odd)
                     def _():
                         pass_on(c).start()
+                        if c + 1 < parts:
+                            far(c + 1).start()
                 else:
                     far(c).wait_recv()
                 block = window[k - 1, piece(c)]
@@ -180,77 +182,70 @@
         pair = merge(pair, (row_box[step, 0:1], row_box[step, 1:2]))
     row_lse = pair[0] + jnp.log2(pair[1])
 
-    def back(k, c):
-        part = text_part.at[k, piece(c)]
+    def stripe(c):
+        return pl.ds(c * strip, strip)
+
+    def back(k, c, onward=True):
+        part = text_part.at[k, stripe(c)]
+        if k == 2 and onward:
+            return remote(part, inbox.at[1, stripe(c)], back_send.at[1, c], back_recv.at[1, c], at(2))
         if k == 2:
-            return (
-                remote(part, inbox.at[1, piece(c)], back_send.at[1, c], back_recv.at[1, c], at(2)),
-                remote(part, relay.at[piece(c)], back_send.at[1, c], back_recv.at[2, c], at(1)),
-            )
-        return remote(part, inbox.at[0, piece(c)], back_send.at[0, c], back_recv.at[0, c], at(1))
-
-    def weights(k):
+            return remote(part, relay.at[stripe(c)], back_send.at[1, c], back_recv.at[2, c], at(1))
+        return remote(part, inbox.at[0, stripe(c)], back_send.at[0, c], back_recv.at[0, c], at(1))
+
+    def column_lse(k):
         pair = (wide[k, 0:1], wide[k, 1:2])
         for other in range(SPAN):
             if other != k:
                 stat_copy(other, k).wait_recv()
                 pair = merge(pair, (col_box[k, other, 0:1], col_box[k, other, 1:2]))
-        col_lse = jnp.broadcast_to(pair[0] + jnp.log2(pair[1]), (LANES, padded)).T
-        for c in range(parts):
-            start = k * cols + c * chunk
-            tile = logits[pl.ds(start, chunk)]
-            own_lse = col_lse[c * chunk:(c + 1) * chunk, 0:1]
-            weight = 0.5 * (jnp.exp2(tile - row_lse) + jnp.exp2(tile - own_lse))
-            if k == 0:
-                here = positive(c)
-                weight = jnp.where(here, weight - 1.0, weight)
-                score = jnp.sum(jnp.where(here, tile, 0.0), axis=1, keepdims=True)
-                own_row = jnp.sum(jnp.where(here, row_lse, 0.0), axis=1, keepdims=True)
-                tall[piece(c)] = ln2 * jnp.where(lane == 0, own_row - score, own_lse - score)
-            high, low = split(weight)
-            g_high[pl.ds(start, chunk)] = high
-            g_low[pl.ds(start, chunk)] = low
+        return jnp.broadcast_to(pair[0] + jnp.log2(pair[1]), (LANES, padded)).T
+
+    def weights(k, c, col_lse):
+        start = k * cols + c * strip
+        tile = logits[pl.ds(start, strip)]
+        own_lse = col_lse[c * strip:(c + 1) * strip, 0:1]
+        weight = 0.5 * (jnp.exp2(tile - row_lse) + jnp.exp2(tile - own_lse))
+        if k == 0:
+            here = positive(c)
+            weight = jnp.where(here, weight - 1.0, weight)
+            score = jnp.sum(jnp.where(here, tile, 0.0), axis=1, keepdims=True)
+            own_row = jnp.sum(jnp.where(here, row_lse, 0.0), axis=1, keepdims=True)
+            lanes = lax.broadcasted_iota(jnp.int32, (strip, LANES), 1)
+            tall[stripe(c)] = jnp.where(lanes == 0, own_row - score, own_lse - score)
+        high, low = split(weight)
+        g_high[pl.ds(start, strip)] = high
+        g_low[pl.ds(start, strip)] = low
 
     def text_terms(k, c):
-        here = pl.ds(k * cols + c * chunk, chunk)
-        return ln2 * dot3(g_high[here], g_low[here], audio_high[...], audio_low[...])
-
-    weights(2)
-    for c in range(parts):
-        text_part[2, piece(c)] = text_terms(2, c)
+        here = pl.ds(k * cols + c * strip, strip)
+        return dot3(g_high[here], g_low[here], audio_high[...], audio_low[...])
+
+    col_lse = column_lse(2)
+    for c in range(steps):
+        weights(2, c, col_lse)
+        text_part[2, stripe(c)] = text_terms(2, c)
 
         @pl.when(odd)
         def _():
-            back(2, c)[0].start()
+            back(2, c).start()
 
         @pl.when(even)
         def _():
-            back(2, c)[1].start()
-
-    weights(1)
-    for c in range(parts):
-        text_part[1, piece(c)] = text_terms(1, c)
-
-        @pl.when(odd)
-        def _():
-            back(2, c)[1].wait_recv()
-            text_part[1, piece(c)] += relay[piece(c)]
-
-        back(1, c).start()
-
-    weights(0)
-    losses = tall[...].T
-    loss_rows[...] = losses[0:1, 0:cols]
-    loss_cols[...] = losses[1:2, 0:cols]
-
-    span = 256 if rows % 256 == 0 else rows
-    for start in range(0, rows, span):
+            back(2, c, False).start()
+
+    for k in (1, 0):
+        col_lse = column_lse(k)
+        for c in range(steps):
+            weights(k, c, col_lse)
+
+    def audio_terms(lanes):
         total = None
         for k in range(SPAN):
-            here = (pl.ds(k * cols, cols), pl.ds(start, span))
+            here = (pl.ds(k * cols, cols), lanes)
             term = dot3(text_turned_high[k], text_turned_low[k], g_high[here], g_low[here])
             total = term if total is None else total + term
-        audio_part[pl.ds(start, span)] = logit_scale * total.T
+        return total.T
 
     def share(group):
         return pl.ds(pl.multiple_of(group * cols, 8), cols)
@@ -261,11 +256,37 @@
             ga_send.at[step], ga_recv.at[step], at(0, peer(step)),
         )
 
-    for step in range(1, n_group):
+    aligned = cols % LANES == 0
+
+    def own_share(step):
+        start = peer(step) * cols
+        audio_part[share(peer(step))] = audio_terms(pl.ds(pl.multiple_of(start, LANES), cols))
+
+    if not aligned:
+        audio_part[...] = audio_terms(pl.ds(0, rows))
+    for step in range(1, n_group):
+        if aligned:
+            own_share(step)
         spread(step).start()
 
-    for c in range(parts):
-        text_part[0, piece(c)] = text_terms(0, c)
+    for c in range(steps):
+        text_part[1, stripe(c)] = text_terms(1, c)
+
+        @pl.when(odd)
+        def _():
+            back(2, c, False).wait_recv()
+            text_part[1, stripe(c)] += relay[stripe(c)]
+
+        back(1, c).start()
+
+    losses = tall[...].T
+    loss_rows[...] = losses[0:1, 0:cols].reshape(loss_rows.shape)
+    loss_cols[...] = losses[1:2, 0:cols].reshape(loss_cols.shape)
+
+    for c in range(steps):
+        text_part[0, stripe(c)] = text_terms(0, c)
+    if aligned:
+        own_share(0)
 
     total = audio_part[share(member)]
     for step in range(1, n_group):
@@ -273,19 +294,21 @@
         total = total + audio_inbox[step]
     grad_audio[...] = total
 
-    for c in range(parts):
+    for c in range(steps):
         back(1, c).wait_recv()
-        grad_text[piece(c)] = text_part[0, piece(c)] + inbox[0, piece(c)]
+        grad_text[stripe(c)] = text_part[0, stripe(c)] + inbox[0, stripe(c)]
 
         @pl.when(odd)
         def _():
-            back(2, c)[0].wait_recv()
-            grad_text[piece(c)] += inbox[1, piece(c)]
+            back(2, c).wait_recv()
+            grad_text[stripe(c)] += inbox[1, stripe(c)]
+
+    for c in range(steps):
+        back(2, c).wait_send()
+        back(1, c).wait_send()
 
     for c in range(parts):
         near(c).wait_send()
-        back(2, c)[0].wait_send()
-        back(1, c).wait_send()
 
         @pl.when(odd)
         def _():
@@ -306,17 +329,17 @@
 def shards(n_blk, n_group, audio_embed, text_embed):
     rows, depth = audio_embed.shape
     cols = text_embed.shape[0]
-    parts = 2
+    parts, steps = 3, 2
     padded = -(-cols // LANES) * LANES
     vmem = pl.BlockSpec(memory_space=pltpu.VMEM)
     dma = pltpu.SemaphoreType.DMA
     grad_audio, grad_text, loss_rows, loss_cols = pl.pallas_call(
-        functools.partial(kernel, n_blk, n_group, parts),
+        functools.partial(kernel, n_blk, n_group, parts, steps),
         out_shape=(
             jax.ShapeDtypeStruct((cols, depth), f32),
             jax.ShapeDtypeStruct((cols, depth), f32),
-            jax.ShapeDtypeStruct((1, cols), f32),
-            jax.ShapeDtypeStruct((1, cols), f32),
+            jax.ShapeDtypeStruct((cols,), f32),
+            jax.ShapeDtypeStruct((cols,), f32),
         ),
         in_specs=[vmem, vmem],
         out_specs=(vmem, vmem, vmem, vmem),
@@ -344,7 +367,7 @@
             dma((3, parts)), dma((2, parts)),
             dma((SPAN, SPAN)), dma((SPAN, SPAN)),
             dma((n_group,)), dma((n_group,)),
-            dma((2, parts)), dma((3, parts)),
+            dma((2, steps)), dma((3, steps)),
             dma((n_group,)), dma((n_group,)),
         ],
         compiler_params=pltpu.CompilerParams(
@@ -352,7 +375,7 @@
         ),
         name="contrast",
     )(audio_embed, text_embed)
-    return grad_audio, grad_text, loss_rows.reshape(cols), loss_cols.reshape(cols)
+    return logit_scale * grad_audio, ln2 * grad_text, ln2 * loss_rows, ln2 * loss_cols
 
 
 def solution(mesh):

time: 68 us -> 63.5 us (0.934)
  local copies, waits for them, and re-layouts: 2.95 us -> 0.01 us
  Pallas kernels: 61.6 us -> 59.3 us
    mul x0 -> x2, other arithmetic: none -> 3.27 us  [the longest x1 2.69 us: shards(): ln2 * grad_text]
    unnamed x4, local copies, waits for them, and re-layouts: 2.95 us -> 0.01 us
    pallas_call x2 -> x0, other arithmetic: 2.6 us -> none  [shards(): pl.pallas_call(functools.partial(kernel, n_blk, n_group, parts), out_shap...]
    pallas_call x1, Pallas kernels: 61.6 us -> 59.3 us  [shards(): pl.pallas_call(functools.partial(kernel, n_blk, n_group, parts, steps), o...]
where the time goes in v2:
time: 63.5 us; the launch traced here: 63.3 us
  Pallas kernels  59.3 us (93%)
  other arithmetic  3.27 us (5%)
  between operations  0.66 us (1%)
    pallas_call x1, Pallas kernels, shards(): pl.pallas_call(functools.partial(kernel, n_blk, n_group, parts, steps), o...  59.3 us
    mul x1, other arithmetic, shards(): ln2 * grad_text  2.69 us

profile of v2, /device:TPU:0, one launch (start us, length us, event | category | flops | bytes accessed | tf_op | source)
XLA Modules:
  0.0 63.3 jit_solution(10751842465370027503)
XLA Ops:
  0.6 59.3 %contrast.1 = (f32[384,512]{1,0:T(8,128)}, f32[384,512]{1,0:T(8,128)}, f32[384]{0:T(512)}, f32[384]{0:T(512)}) custom-call(f32[768,512]{1,0:T(8,128)} %audio.1, f32[384,512]{1,0:T(8,128)} %text.1), custom_call_target="tpu_custom_call" | custom-call | tf_op jit(solution)/shard_map/contrast/pallas_call | solution.py:336
  60.0 0.0 copy-start
  60.0 0.0 copy-start.1
  60.0 2.7 %broadcast_multiply_fusion = (f32[384,512]{1,0:T(8,128)}, f32[384,512]{1,0:T(8,128)}) fusion(f32[384,512]{1,0:T(8,128)} %get-tuple-element.9, f32[384,512]{1,0:T(8,128)} %get-tuple-element.8), kind=kLoop, calls=%fused_computation | loop fusion | flops 393216 | bytes 3145728 | tf_op jit(solution)/shard_map/mul | solution.py:378
  62.7 0.0 copy-done
  62.7 0.0 copy-done.1
  62.7 0.6 broadcast_multiply_fusion.2
Async XLA Ops:
  60.0 2.7 %copy-start = (f32[384]{0:T(512)S(1)}, f32[384]{0:T(512)}, u32[]{:S(2)}) copy-start(f32[384]{0:T(512)} %get-tuple-element.10) | copy-start | bytes 4612
  60.0 2.7 %copy-start.1 = (f32[384]{0:T(512)S(1)}, f32[384]{0:T(512)}, u32[]{:S(2)}) copy-start(f32[384]{0:T(512)} %get-tuple-element.11) | copy-start | bytes 4612

commit v3 on v2

--- a/solution.py
+++ b/solution.py
@@ -42,15 +42,16 @@
 
 def kernel(
     n_blk, n_group, parts, steps,
-    audio, text,
+    audio_hbm, text_hbm,
     grad_audio, grad_text, loss_rows, loss_cols,
     window, audio_high, audio_low, turned_high, turned_low,
     text_turned_high, text_turned_low, logits, g_high, g_low,
     audio_part, audio_inbox,
     text_part, inbox, relay,
+    audio, text, col_term,
     tall, wide, col_box, row_box, row_stat,
     fwd_send, fwd_recv, stat_send, stat_recv, row_send, row_recv,
-    back_send, back_recv, ga_send, ga_recv,
+    back_send, back_recv, ga_send, ga_recv, load_sem,
 ):
     rows, depth = audio.shape
     cols = text.shape[0]
@@ -76,6 +77,13 @@
         pl.semaphore_signal(barrier, inc=1, device_id=at(step), device_id_type=MESH)
     for step in range(1, n_group):
         pl.semaphore_signal(barrier, inc=1, device_id=at(0, peer(step)), device_id_type=MESH)
+    loads = (
+        pltpu.make_async_copy(text_hbm, text, load_sem.at[0]),
+        pltpu.make_async_copy(audio_hbm, audio, load_sem.at[1]),
+    )
+    for load in loads:
+        load.start()
+    loads[0].wait()
     pl.semaphore_wait(barrier, 4 + n_group - 1)
 
     def piece(c):
@@ -100,6 +108,7 @@
 
     for c in range(parts):
         near(c).start()
+    loads[1].wait()
     scaled = audio[...] * (logit_scale * log2e)
     high, low = split(scaled)
     audio_high[...] = high
@@ -174,6 +183,33 @@
         text_turned_high[k] = high
         text_turned_low[k] = low
 
+    def stripe(c):
+        return pl.ds(c * strip, strip)
+
+    def back(k, c, onward=True):
+        part = text_part.at[k, stripe(c)]
+        if k == 2 and onward:
+            return remote(part, inbox.at[1, stripe(c)], back_send.at[1, c], back_recv.at[1, c], at(2))
+        if k == 2:
+            return remote(part, relay.at[stripe(c)], back_send.at[1, c], back_recv.at[2, c], at(1))
+        return remote(part, inbox.at[0, stripe(c)], back_send.at[0, c], back_recv.at[0, c], at(1))
+
+    def column_lse(k):
+        pair = (wide[k, 0:1], wide[k, 1:2])
+        for other in range(SPAN):
+            if other != k:
+                stat_copy(other, k).wait_recv()
+                pair = merge(pair, (col_box[k, other, 0:1], col_box[k, other, 1:2]))
+        return jnp.broadcast_to(pair[0] + jnp.log2(pair[1]), (LANES, padded)).T
+
+    def column_part(k, c, col_lse):
+        tile = logits[pl.ds(k * cols + c * strip, strip)]
+        return jnp.exp2(tile - col_lse[c * strip:(c + 1) * strip, 0:1])
+
+    col_lse = column_lse(2)
+    for c in range(steps):
+        col_term[stripe(c)] = column_part(2, c, col_lse)
+
     pair = (row_stat[0:1], row_stat[1:2])
     for step in range(1, n_group):
         remote(
@@ -182,31 +218,13 @@
         pair = merge(pair, (row_box[step, 0:1], row_box[step, 1:2]))
     row_lse = pair[0] + jnp.log2(pair[1])
 
-    def stripe(c):
-        return pl.ds(c * strip, strip)
-
-    def back(k, c, onward=True):
-        part = text_part.at[k, stripe(c)]
-        if k == 2 and onward:
-            return remote(part, inbox.at[1, stripe(c)], back_send.at[1, c], back_recv.at[1, c], at(2))
-        if k == 2:
-            return remote(part, relay.at[stripe(c)], back_send.at[1, c], back_recv.at[2, c], at(1))
-        return remote(part, inbox.at[0, stripe(c)], back_send.at[0, c], back_recv.at[0, c], at(1))
-
-    def column_lse(k):
-        pair = (wide[k, 0:1], wide[k, 1:2])
-        for other in range(SPAN):
-            if other != k:
-                stat_copy(other, k).wait_recv()
-                pair = merge(pair, (col_box[k, other, 0:1], col_box[k, other, 1:2]))
-        return jnp.broadcast_to(pair[0] + jnp.log2(pair[1]), (LANES, padded)).T
-
     def weights(k, c, col_lse):
         start = k * cols + c * strip
         tile = logits[pl.ds(start, strip)]
-        own_lse = col_lse[c * strip:(c + 1) * strip, 0:1]
-        weight = 0.5 * (jnp.exp2(tile - row_lse) + jnp.exp2(tile - own_lse))
+        by_column = col_term[stripe(c)] if k == 2 else column_part(k, c, col_lse)
+        weight = 0.5 * (jnp.exp2(tile - row_lse) + by_column)
         if k == 0:
+            own_lse = col_lse[c * strip:(c + 1) * strip, 0:1]
             here = positive(c)
             weight = jnp.where(here, weight - 1.0, weight)
             score = jnp.sum(jnp.where(here, tile, 0.0), axis=1, keepdims=True)
@@ -221,7 +239,6 @@
         here = pl.ds(k * cols + c * strip, strip)
         return dot3(g_high[here], g_low[here], audio_high[...], audio_low[...])
 
-    col_lse = column_lse(2)
     for c in range(steps):
         weights(2, c, col_lse)
         text_part[2, stripe(c)] = text_terms(2, c)
@@ -250,24 +267,30 @@
     def share(group):
         return pl.ds(pl.multiple_of(group * cols, 8), cols)
 
-    def spread(step):
+    slices = cols // LANES if cols % LANES == 0 else 1
+    width = cols // slices
+
+    def spread(step, lot):
+        start = peer(step) * cols + lot * width
         return remote(
-            audio_part.at[share(peer(step))], audio_inbox.at[step],
-            ga_send.at[step], ga_recv.at[step], at(0, peer(step)),
+            audio_part.at[pl.ds(pl.multiple_of(start, 8), width)],
+            audio_inbox.at[step, pl.ds(lot * width, width)],
+            ga_send.at[step, lot], ga_recv.at[step, lot], at(0, peer(step)),
         )
 
     aligned = cols % LANES == 0
 
-    def own_share(step):
-        start = peer(step) * cols
-        audio_part[share(peer(step))] = audio_terms(pl.ds(pl.multiple_of(start, LANES), cols))
+    def own_share(step, lot):
+        start = pl.multiple_of(peer(step) * cols + lot * width, width)
+        audio_part[pl.ds(start, width)] = audio_terms(pl.ds(start, width))
 
     if not aligned:
         audio_part[...] = audio_terms(pl.ds(0, rows))
     for step in range(1, n_group):
-        if aligned:
-            own_share(step)
-        spread(step).start()
+        for lot in range(slices):
+            if aligned:
+                own_share(step, lot)
+            spread(step, lot).start()
 
     for c in range(steps):
         text_part[1, stripe(c)] = text_terms(1, c)
@@ -286,13 +309,16 @@
     for c in range(steps):
         text_part[0, stripe(c)] = text_terms(0, c)
     if aligned:
-        own_share(0)
-
-    total = audio_part[share(member)]
-    for step in range(1, n_group):
-        spread(step).wait_recv()
-        total = total + audio_inbox[step]
-    grad_audio[...] = total
+        start = pl.multiple_of(member * cols, cols)
+        audio_part[share(member)] = audio_terms(pl.ds(start, cols))
+
+    for lot in range(slices):
+        rank = pl.ds(lot * width, width)
+        total = audio_part[pl.ds(pl.multiple_of(member * cols + lot * width, 8), width)]
+        for step in range(1, n_group):
+            spread(step, lot).wait_recv()
+            total = total + audio_inbox[step, rank]
+        grad_audio[rank] = total
 
     for c in range(steps):
         back(1, c).wait_recv()
@@ -323,7 +349,8 @@
         remote(
             row_stat, row_box.at[step], row_send.at[step], row_recv.at[step], at(0, peer(step))
         ).wait_send()
-        spread(step).wait_send()
+        for lot in range(slices):
+            spread(step, lot).wait_send()
 
 
 def shards(n_blk, n_group, audio_embed, text_embed):
@@ -331,6 +358,7 @@
     cols = text_embed.shape[0]
     parts, steps = 3, 2
     padded = -(-cols // LANES) * LANES
+    slices = cols // LANES if cols % LANES == 0 else 1
     vmem = pl.BlockSpec(memory_space=pltpu.VMEM)
     dma = pltpu.SemaphoreType.DMA
     grad_audio, grad_text, loss_rows, loss_cols = pl.pallas_call(
@@ -341,7 +369,7 @@
             jax.ShapeDtypeStruct((cols,), f32),
             jax.ShapeDtypeStruct((cols,), f32),
         ),
-        in_specs=[vmem, vmem],
+        in_specs=[pl.BlockSpec(memory_space=pltpu.HBM)] * 2,
         out_specs=(vmem, vmem, vmem, vmem),
         scratch_shapes=[
             pltpu.VMEM((SPAN - 1, cols, depth), f32),
@@ -359,6 +387,9 @@
             pltpu.VMEM((SPAN, cols, depth), f32),
             pltpu.VMEM((2, cols, depth), f32),
             pltpu.VMEM((cols, depth), f32),
+            pltpu.VMEM((rows, depth), f32),
+            pltpu.VMEM((cols, depth), f32),
+            pltpu.VMEM((cols, rows), f32),
             pltpu.VMEM((padded, LANES), f32),
             pltpu.VMEM((SPAN, 8, padded), f32),
             pltpu.VMEM((SPAN, SPAN, 8, padded), f32),
@@ -368,10 +399,10 @@
             dma((SPAN, SPAN)), dma((SPAN, SPAN)),
             dma((n_group,)), dma((n_group,)),
             dma((2, steps)), dma((3, steps)),
-            dma((n_group,)), dma((n_group,)),
+            dma((n_group, slices)), dma((n_group, slices)), dma((2,)),
         ],
         compiler_params=pltpu.CompilerParams(
-            collective_id=0, has_side_effects=True, vmem_limit_bytes=56 * 1024 * 1024
+            collective_id=0, has_side_effects=True, vmem_limit_bytes=36 * 1024 * 1024
         ),
         name="contrast",
     )(audio_embed, text_embed)

time: 63.5 us -> 60.5 us (0.953)
  Pallas kernels: 59.3 us -> 55.3 us
  local copies, waits for them, and re-layouts: 0.01 us -> 2.53 us
  other arithmetic: 3.27 us -> 1.9 us
    pallas_call x1, Pallas kernels: 59.3 us -> 55.3 us  [shards(): pl.pallas_call(functools.partial(kernel, n_blk, n_group, parts, steps), o...]
    unnamed x4, local copies, waits for them, and re-layouts: 0.01 us -> 2.53 us
    mul x1, other arithmetic: 2.69 us -> 1.32 us  [shards(): ln2 * grad_text]
where the time goes in v3:
time: 60.5 us; the launch traced here: 60.4 us
  Pallas kernels  55.3 us (91%)
  local copies, waits for them, and re-layouts  2.53 us (4%)
  other arithmetic  1.9 us (3%)
  between operations  0.65 us (1%)
    pallas_call x1, Pallas kernels, shards(): pl.pallas_call(functools.partial(kernel, n_blk, n_group, parts, steps), o...  55.3 us
    unnamed x4, local copies, waits for them, and re-layouts  2.53 us
    mul x1, other arithmetic, shards(): ln2 * grad_text  1.32 us

profile of v3, /device:TPU:0, one launch (start us, length us, event | category | flops | bytes accessed | tf_op | source)
XLA Modules:
  0.0 60.4 jit_solution(13282518100430732301)
XLA Ops:
  0.6 0.0 copy-start
  0.6 1.4 %copy-done = f32[768,512]{1,0:T(8,128)S(1)} copy-done((f32[768,512]{1,0:T(8,128)S(1)}, f32[768,512]{1,0:T(8,128)}, u32[]{:S(2)}) %copy-start) | copy-done | bytes 1572888
  2.0 0.0 copy-start.1
  2.0 1.1 %copy-done.1 = f32[384,512]{1,0:T(8,128)S(1)} copy-done((f32[384,512]{1,0:T(8,128)S(1)}, f32[384,512]{1,0:T(8,128)}, u32[]{:S(2)}) %copy-start.1) | copy-done | bytes 786456
  3.2 55.3 %contrast.1 = (f32[384,512]{1,0:T(8,128)S(1)}, f32[384,512]{1,0:T(8,128)S(1)}, f32[384]{0:T(512)S(1)}, f32[384]{0:T(512)S(1)}) custom-call(f32[768,512]{1,0:T(8,128)S(1)} %copy-done, f32[384,512]{1,0:T(8,128)S(1)} %copy-done.1), custom_call_target="tpu_custom_call" | custom-call | tf_op jit(solution)/shard_map/contrast/pallas_call | solution.py:364
  58.5 1.3 %broadcast_multiply_fusion = (f32[384,512]{1,0:T(8,128)}, f32[384,512]{1,0:T(8,128)}) fusion(f32[384,512]{1,0:T(8,128)S(1)} %get-tuple-element.9, f32[384,512]{1,0:T(8,128)S(1)} %get-tuple-element.8), kind=kLoop, calls=%fused_computation | loop fusion | flops 393216 | bytes 3145728 | tf_op jit(solution)/shard_map/mul | solution.py:409
  59.8 0.6 broadcast_multiply_fusion.2
Async XLA Ops:
  0.6 1.4 %copy-start = (f32[768,512]{1,0:T(8,128)S(1)}, f32[768,512]{1,0:T(8,128)}, u32[]{:S(2)}) copy-start(f32[768,512]{1,0:T(8,128)} %audio_hbm.1) | copy-start | bytes 4718596
  2.0 1.1 %copy-start.1 = (f32[384,512]{1,0:T(8,128)S(1)}, f32[384,512]{1,0:T(8,128)}, u32[]{:S(2)}) copy-start(f32[384,512]{1,0:T(8,128)} %text_hbm.1) | copy-start | bytes 2359300

commit v4 on v3

--- a/solution.py
+++ b/solution.py
@@ -402,7 +402,7 @@
             dma((n_group, slices)), dma((n_group, slices)), dma((2,)),
         ],
         compiler_params=pltpu.CompilerParams(
-            collective_id=0, has_side_effects=True, vmem_limit_bytes=36 * 1024 * 1024
+            collective_id=0, has_side_effects=True, vmem_limit_bytes=53 * 1024 * 1024
         ),
         name="contrast",
     )(audio_embed, text_embed)

time: 60.5 us -> 60.1 us (level)
  local copies, waits for them, and re-layouts: 2.53 us -> 0 us
  other arithmetic: 1.9 us -> 3.03 us
  Pallas kernels: 55.3 us -> 56.2 us
    unnamed x4 -> x0, local copies, waits for them, and re-layouts: 2.53 us -> none
    mul x1, other arithmetic: 1.32 us -> 2.45 us  [shards(): ln2 * grad_text]
    pallas_call x1, Pallas kernels: 55.3 us -> 56.2 us  [shards(): pl.pallas_call(functools.partial(kernel, n_blk, n_group, parts, steps), o...]
where the time goes in v4:
time: 60.1 us; the launch traced here: 59.9 us
  Pallas kernels  56.2 us (94%)
  other arithmetic  3.03 us (5%)
  between operations  0.64 us (1%)
    pallas_call x1, Pallas kernels, shards(): pl.pallas_call(functools.partial(kernel, n_blk, n_group, parts, steps), o...  56.2 us
    mul x1, other arithmetic, shards(): ln2 * grad_text  2.45 us

profile of v4, /device:TPU:0, one launch (start us, length us, event | category | flops | bytes accessed | tf_op | source)
XLA Modules:
  0.0 59.9 jit_solution(3422563582861907522)
XLA Ops:
  0.6 56.2 %contrast.1 = (f32[384,512]{1,0:T(8,128)S(1)}, f32[384,512]{1,0:T(8,128)}, f32[384]{0:T(512)S(1)}, f32[384]{0:T(512)S(1)}) custom-call(f32[768,512]{1,0:T(8,128)} %audio_hbm.1, f32[384,512]{1,0:T(8,128)} %text_hbm.1), custom_call_target="tpu_custom_call" | custom-call | tf_op jit(solution)/shard_map/contrast/pallas_call | solution.py:364
  56.9 2.5 %broadcast_multiply_fusion = (f32[384,512]{1,0:T(8,128)}, f32[384,512]{1,0:T(8,128)}) fusion(f32[384,512]{1,0:T(8,128)} %get-tuple-element.9, f32[384,512]{1,0:T(8,128)S(1)} %get-tuple-element.8), kind=kLoop, calls=%fused_computation | loop fusion | flops 393216 | bytes 3145728 | tf_op jit(solution)/shard_map/mul | solution.py:409
  59.3 0.6 broadcast_multiply_fusion.2
